TPU v7x, 512 devices: a whole 4x4x16 slice. The times are simulated.
512 devices in a mesh: sec: 4 (over z_hi, core), gx: 32 (over y, z_lo), gy: 4 (over x).
Axes of the slice: x: 4, y: 4, z: 16 (z_hi: 2, z_lo: 8; z = z_hi * 8 + z_lo), core: 2. Of those that a mesh axis runs over, the one named last changes fastest.
Arguments:
- adjoint: float32 [4, 5, 256, 32, 128], P('sec', None, 'gx', 'gy'), may hold values from -6 to 6
- flow: float32 [4, 6, 256, 32, 128], P('sec', None, 'gx', 'gy'), as said below
- point_cell: int32 [4, 32, 4, 1024], P('sec', 'gx', 'gy'), may hold values from 0 to 8191
- point_dest: int32 [4, 32, 4, 1024], P('sec', 'gx', 'gy'), may hold values from 0 to 127, as said below
- point_target: int32 [4, 32, 4, 1024], P('sec', 'gx', 'gy'), may hold values from 0 to 8191
- point_weight: float32 [4, 32, 4, 1024], P('sec', 'gx', 'gy'), may hold values from 0.5 to 2
- point_count: int32 [4, 32, 4], P('sec', 'gx', 'gy'), may hold values from 0 to 1024, as said below
Outputs:
- adjoint_next: float32 [4, 5, 256, 32, 128], P('sec', None, 'gx', 'gy')
Inputs may be any that keep to these rules, and one draw needn't show every extreme that they name: `flow`: density 0.6 to 1.6, pressure 0.4 (E - kinetic) from 0.5 to 1.5, sponge rate 0.05 to 1. `point_count`: zero on the near-field section; on far-field tiles a multiple of 128, reaching 1024 on some tile. `point_dest`: among the live slots of one far-field tile at most 20 name the same near-field tile, and 20 is reached. Near-field tiles receive unequal numbers of points.
All inputs are finite; a program needn't handle non-finite values.
Results may differ from a plain program's by a relative error of at most 0.00002.
Values sent between devices are 32-bit elements; how exact they have to be, the bound alone decides.
A program may use at most 64 MiB of HBM per device.

v0:
```python
import jax
import jax.numpy as jnp
from jax import lax
from jax.sharding import PartitionSpec as P

GAMMA_MINUS = 0.4
GAMMA_RATIO = 1.4
STEP_SIZE = 0.4


def extended(x, sides, width):
    for axis, dim in sides:
        count, length = (lax.axis_size(axis), x.shape[dim])
        up = [(i, (i + 1) % count) for i in range(count - 1)]
        down = [(j, i) for i, j in up]
        last = lax.slice_in_dim(x, length - width, length, axis=dim)
        initial = lax.slice_in_dim(x, 0, width, axis=dim)
        before = lax.ppermute(last, axis, up)
        after = lax.ppermute(initial, axis, down)
        x = jnp.concatenate([before, x, after], axis=dim)
    return x


def shifted(padded, offset, along):
    length = padded.shape[along] - 6
    return lax.slice_in_dim(padded, 3 + offset, 3 + offset + length, axis=along)


def stencil(padded, along):
    first = shifted(padded, 1, along) - shifted(padded, -1, along)
    second = shifted(padded, 2, along) - shifted(padded, -2, along)
    third = shifted(padded, 3, along) - shifted(padded, -3, along)
    return (45.0 * first - 9.0 * second + third) / 60.0


def wrap_last(values_in):
    return jnp.concatenate([values_in[..., -3:], values_in, values_in[..., :3]], axis=-1)


def fluxes(adjoint, flow, direction):
    density = flow[0]
    inverse = 1.0 / density
    momenta = flow[1:4]
    velocity = momenta[direction] * inverse
    kinetic = (
        0.5
        * (momenta[0] * momenta[0] + momenta[1] * momenta[1] + momenta[2] * momenta[2])
        * inverse
    )
    pressure = GAMMA_MINUS * (flow[4] - kinetic)
    stiffness = GAMMA_RATIO * pressure
    return jnp.stack(
        [
            velocity * adjoint[0],
            velocity * adjoint[1],
            velocity * adjoint[2],
            velocity * adjoint[3],
            velocity * adjoint[4],
            density * adjoint[0] + stiffness * adjoint[4],
            adjoint[1 + direction] * inverse,
        ]
    )


def masked_fluxes(adjoint, flow, direction, inside):
    safe_flow = jnp.concatenate([jnp.where(inside, flow[:1], 1.0), flow[1:]], axis=0)
    return jnp.where(inside, fluxes(adjoint, safe_flow, direction), 0.0)


def assemble(adjoint, flow, along_x, along_y, along_z, source):
    summed = along_x + along_y + along_z
    rate_list = jnp.stack(
        [
            summed[0],
            summed[1] + along_x[5],
            summed[2] + along_y[5],
            summed[3] + along_z[5],
            summed[4] + summed[6],
        ]
    )
    return adjoint + STEP_SIZE * (rate_list - flow[5] * adjoint + source)


def local(adjoint, flow, point_cell, point_dest, point_target, point_weight, point_count):
    adjoint_block = adjoint[0]
    fields = flow[0]
    channels, rows_x, rows_y, depth_cells = adjoint_block.shape
    tile_count = lax.axis_size("gx") * lax.axis_size("gy")
    slot_count = point_cell.shape[-1]
    capacity = 5 * slot_count // (2 * tile_count)
    buffer_width = tile_count * capacity
    cell_index = point_cell.reshape(slot_count)
    dest_tile = point_dest.reshape(slot_count)
    target_cell = point_target.reshape(slot_count)
    flat_block = adjoint_block.reshape(channels, -1)
    values = flat_block[:, cell_index] * point_weight.reshape(slot_count)[None, :]
    live_slot = jnp.arange(slot_count, dtype=jnp.int32) < point_count.reshape(())
    onehot = (
        (dest_tile[:, None] == jnp.arange(tile_count, dtype=jnp.int32)[None, :])
        & live_slot[:, None]
    ).astype(jnp.int32)
    slot_rank = jnp.sum(jnp.cumsum(onehot, axis=0) * onehot, axis=1) - 1
    position = jnp.where(live_slot, dest_tile * capacity + slot_rank, buffer_width)
    packed_values = (
        jnp.zeros((channels, buffer_width), jnp.float32).at[:, position].set(values, mode="drop")
    )
    packed_targets = (
        jnp.zeros((1, buffer_width), jnp.int32).at[0, position].set(target_cell, mode="drop")
    )
    tile_values, tile_targets = (
        lax.all_to_all(packed_values, ("gx", "gy"), split_axis=1, concat_axis=1, tiled=True),
        lax.all_to_all(packed_targets, ("gx", "gy"), split_axis=1, concat_axis=1, tiled=True),
    )
    merged_values, merged_targets = (
        lax.all_gather(tile_values, "sec", axis=1, tiled=True),
        lax.all_gather(tile_targets, "sec", axis=1, tiled=True),
    )
    source = jnp.zeros((channels, rows_x * rows_y * depth_cells), jnp.float32)
    source = (
        source.at[:, merged_targets[0]]
        .add(merged_values)
        .reshape(channels, rows_x, rows_y, depth_cells)
    )
    is_near = lax.axis_index("sec") == lax.axis_size("sec") - 1
    source = jnp.where(is_near, source, 0.0)
    joined = jnp.concatenate([adjoint_block, fields], axis=0)
    padded = extended(joined, (("gx", 1), ("gy", 2)), 3)
    x_position = lax.axis_index("gx") * rows_x - 3 + jnp.arange(rows_x + 6, dtype=jnp.int32)
    x_inside = (x_position >= 0) & (x_position < lax.axis_size("gx") * rows_x)
    y_position = lax.axis_index("gy") * rows_y - 3 + jnp.arange(rows_y + 6, dtype=jnp.int32)
    y_inside = (y_position >= 0) & (y_position < lax.axis_size("gy") * rows_y)
    strip_x = padded[:, :, 3:-3, :]
    flux_x = masked_fluxes(strip_x[:channels], strip_x[channels:], 0, x_inside[:, None, None])
    along_x = stencil(flux_x, 1)
    strip_y = padded[:, 3:-3, :, :]
    flux_y = masked_fluxes(strip_y[:channels], strip_y[channels:], 1, y_inside[None, :, None])
    along_y = stencil(flux_y, 2)
    along_z = stencil(wrap_last(fluxes(adjoint_block, fields, 2)), 3)
    result = assemble(adjoint_block, fields, along_x, along_y, along_z, source)
    return result[None]


def solution(mesh):
    placed = (
        P("sec", None, "gx", "gy", None),
        P("sec", None, "gx", "gy", None),
        P("sec", "gx", "gy", None),
        P("sec", "gx", "gy", None),
        P("sec", "gx", "gy", None),
        P("sec", "gx", "gy", None),
        P("sec", "gx", "gy"),
    )
    return jax.shard_map(
        local,
        mesh=mesh,
        in_specs=placed,
        out_specs=P("sec", None, "gx", "gy", None),
        check_vma=False,
    )
```

profile of v0, /device:TPU:91, one launch (start us, length us, event | category | flops | bytes accessed | tf_op | source)
XLA Modules:
  0.0 204.8 jit_solution(14550307588079525748)
XLA Ops:
  0.0 0.0 copy-start.1
  0.0 0.0 copy-start
  0.0 0.0 copy-start.2
  0.0 0.8 copy.17
  1.5 0.3 fusion.6
  2.0 0.0 copy-start.3
  2.0 0.1 copy.18
  2.1 1.2 fusion.4
  3.3 0.7 compare_select_fusion.2
  4.0 0.8 and_reduce_fusion
  4.8 0.7 fusion.72
  5.6 4.5 %scatter_custom_fusion.2 = s32[2560]{0:T(1024)S(1)} fusion(s32[1024]{0:T(1024)S(1)} %broadcast_select_fusion.3, s32[1024]{0:T(1024)} %bitcast.146, s32[]{:T(128)} %constant.27.clone.1), kind=kCustom, calls=%fused_computation.167 | custom fusion | bytes 10752
  10.0 0.7 all_to_all.16
  10.8 18.3 %all-to-all-start = ((s32[1,128,20]{2,0,1:T(1,128)}), s32[1,128,20]{2,0,1:T(1,128)S(1)}, u32[]{:S(2)}, u32[]{:S(2)}) async-start(s32[1,128,20]{2,0,1:T(1,128)} %bitcast.26), calls=%async_computation | async-start | bytes 131072 | tf_op jit(solution)/shard_map/all_to_all | solution.py:112
  29.1 1.6 pad_maximum_fusion.4
  30.7 2.2 %collective-permute-start.1 = (f32[11,3,8,128]{3,2,1,0:T(8,128)}, f32[11,3,8,128]{3,2,1,0:T(8,128)S(1)}, u32[]{:S(2)}, u32[]{:S(2)}) collective-permute-start(f32[11,3,8,128]{3,2,1,0:T(8,128)} %get-tuple-element.18), channel_id=1, source_target_pairs={{4,0},{8,4},{12,8},{16,12},{20,16},{24,20},{28,24},{32,28},{36,32}... | collective-permute-start | bytes 405512 | tf_op jit(solution)/shard_map/ppermute | solution.py:19
  32.8 3.1 %collective-permute-start = (f32[11,3,8,128]{3,2,1,0:T(8,128)S(1)}, f32[11,3,8,128]{3,2,1,0:T(8,128)S(1)}, u32[]{:S(2)}, u32[]{:S(2)}) collective-permute-start(f32[11,3,8,128]{3,2,1,0:T(8,128)S(1)} %get-tuple-element.17), channel_id=1, source_target_pairs={{0,4},{4,8},{8,12},{12,16},{16,20},{20,24},{24,28},{28,32},{32,36}... | collective-permute-start | bytes 405512 | tf_op jit(solution)/shard_map/ppermute | solution.py:18
  36.0 0.0 copy-done.1
  36.0 0.0 copy-done
  36.0 0.0 copy-done.2
  36.2 0.1 fusion.81
  36.3 2.7 %copy.20 = f32[1,5,8,8,128]{1,4,3,2,0:T(8,128)} copy(f32[1,5,8,8,128]{4,3,2,1,0:T(8,128)S(1)} %copy-done) | data formatting | bytes 327680 | tf_op args[0]
  39.0 0.0 copy-done.3
  39.0 9.7 %scatter_custom_fusion = f32[5,2560]{0,1:T(8,128)S(1)} fusion(s32[1024]{0:T(1024)S(1)} %bitcast.142, f32[]{:T(128)} %constant.32.clone.1, f32[1024]{0:T(1024)S(1)} %bitcast.145, f32[5,8192]{0,1:T(8,128)} %bitcast.136, s32[1024]{0:T(1024)S(1)} %broadcast_clamp_fusion), kind=kCustom, calls=%fused_computation.7 | custom fusion | flops 5120 | bytes 223236 | tf_op jit(solution)/shard_map/scatter | solution.py:105
  48.7 0.4 copy.21
  49.1 0.4 all_to_all.19
  49.5 1.0 copy.22
  50.5 0.0 all-to-all-done
  50.5 23.5 %all-to-all-start.1 = ((f32[5,128,20]{2,0,1:T(8,128)}), f32[5,128,20]{2,0,1:T(8,128)S(1)}, u32[]{:S(2)}, u32[]{:S(2)}) async-start(f32[5,128,20]{2,0,1:T(8,128)} %copy.22), calls=%async_computation.1 | async-start | bytes 1048576 | tf_op jit(solution)/shard_map/all_to_all | solution.py:111
  74.0 0.6 broadcast.293
  74.6 0.8 reduce.7
  75.5 0.1 all_to_all.18
  75.6 27.9 %all_gather.6 = s32[1,10240]{1,0:T(1,128)S(1)} all-gather(s32[1,2560]{1,0:T(1,128)S(1)} %all_to_all.18), channel_id=1, replica_groups=mesh['sec'=4,'gx'=32,'gy'=4] {'sec'}, dimensions={1}, use_global_device_ids=true | all-gather | bytes 51200 | tf_op jit(solution)/shard_map/all_gather | solution.py:116
  103.5 0.0 collective-permute-done.1
  103.5 0.0 collective-permute-done
  103.6 0.9 fusion.80
  104.5 2.2 %collective-permute-start.3 = (f32[11,14,3,128]{3,2,1,0:T(4,128)}, f32[11,14,3,128]{3,2,1,0:T(4,128)S(1)}, u32[]{:S(2)}, u32[]{:S(2)}) collective-permute-start(f32[11,14,3,128]{3,2,1,0:T(4,128)} %get-tuple-element.16), channel_id=1, source_target_pairs={{1,0},{2,1},{3,2},{5,4},{6,5},{7,6},{9,8},{10,9},{11,10},{13,12},{... | collective-permute-start | bytes 709640 | tf_op jit(solution)/shard_map/ppermute | solution.py:19
  106.7 3.3 %collective-permute-start.2 = (f32[11,14,3,128]{3,2,1,0:T(4,128)}, f32[11,14,3,128]{3,2,1,0:T(4,128)S(1)}, u32[]{:S(2)}, u32[]{:S(2)}) collective-permute-start(f32[11,14,3,128]{3,2,1,0:T(4,128)} %get-tuple-element.15), channel_id=1, source_target_pairs={{0,1},{1,2},{2,3},{4,5},{5,6},{6,7},{8,9},{9,10},{10,11},{12,13},{... | collective-permute-start | bytes 709640 | tf_op jit(solution)/shard_map/ppermute | solution.py:18
  110.0 0.1 multiply_dynamic-update-slice_fusion.6
  110.2 0.1 fusion.57
  110.3 0.1 multiply_dynamic-update-slice_fusion.3
  110.3 0.1 broadcast_select_fusion.2
  110.5 0.0 all-to-all-done.1
  110.5 0.1 copy.23
  110.5 0.2 all_to_all.21
  110.8 17.0 %all_gather.7 = f32[5,10240]{1,0:T(8,128)S(1)} all-gather(f32[5,2560]{1,0:T(8,128)S(1)} %all_to_all.21), channel_id=1, replica_groups=mesh['sec'=4,'gx'=32,'gy'=4] {'sec'}, dimensions={1}, use_global_device_ids=true | all-gather | bytes 256000 | tf_op jit(solution)/shard_map/all_gather | solution.py:115
  127.7 3.1 %copy.24 = f32[10240,5]{1,0:T(8,128)} copy(f32[10240,5]{0,1:T(8,128)S(1)} %bitcast.138) | data formatting | bytes 409600 | tf_op jit(solution)/shard_map/all_gather | solution.py:115
  130.9 66.5 %scatter_custom_fusion.1 = f32[5,8192]{0,1:T(8,128)} fusion(s32[10240]{0:T(1024)S(1)} %bitcast.139, f32[10240,5]{1,0:T(8,128)} %copy.24, f32[]{:T(128)} %constant.32.clone.1), kind=kCustom, calls=%fused_computation.5 | custom fusion | flops 51200 | bytes 164352 | tf_op jit(solution)/shard_map/scatter-add | solution.py:121
  197.3 2.3 %broadcast_select_fusion = f32[5,8192]{0,1:T(8,128)} fusion(f32[5,8192]{0,1:T(8,128)} %scatter_custom_fusion.1, pred[]{:T(512)S(6)} %eq.28), kind=kLoop, calls=%fused_computation.4 | loop fusion | flops 40960 | bytes 327681 | tf_op jit(solution)/shard_map/jit(_where)/select_n | solution.py:125
  199.6 2.9 %copy.25 = f32[1,5,8,8,128]{4,3,2,1,0:T(8,128)S(1)} copy(f32[1,5,8,8,128]{1,4,3,2,0:T(8,128)} %bitcast.137) | data formatting | bytes 327680 | tf_op jit(solution)/shard_map/jit(_where)/select_n | solution.py:125
  202.5 0.0 collective-permute-done.3
  202.5 0.0 collective-permute-done.2
  202.5 0.1 multiply_dynamic-update-slice_fusion.2
  202.6 0.1 fusion.49
  202.7 0.1 multiply_dynamic-update-slice_fusion.1
  202.8 0.1 fusion.48
  202.9 0.1 fusion.47
  203.0 0.1 fusion.44
  203.1 0.1 multiply_dynamic-update-slice_fusion
  203.2 0.1 broadcast_select_fusion.1
  203.3 0.7 add_add_fusion
  204.1 0.7 multiply_add_fusion
  (31 shorter events, 0.4 us)
Async XLA Ops:
  0.0 36.0 %copy-start.1 = (f32[1,6,8,8,128]{4,3,2,1,0:T(8,128)S(1)}, f32[1,6,8,8,128]{4,3,2,1,0:T(8,128)}, u32[]{:S(2)}) copy-start(f32[1,6,8,8,128]{4,3,2,1,0:T(8,128)} %param.8) | copy-start | bytes 589828
  0.0 36.0 %copy-start = (f32[1,5,8,8,128]{4,3,2,1,0:T(8,128)S(1)}, f32[1,5,8,8,128]{4,3,2,1,0:T(8,128)}, u32[]{:S(2)}) copy-start(f32[1,5,8,8,128]{4,3,2,1,0:T(8,128)} %param.7) | copy-start | bytes 491524
  0.0 36.0 %copy-start.2 = (s32[1,1,1,1024]{3,2,1,0:T(1,128)S(1)}, s32[1,1,1,1024]{3,2,1,0:T(1,128)}, u32[]{:S(2)}) copy-start(s32[1,1,1,1024]{3,2,1,0:T(1,128)} %param.9) | copy-start | bytes 12292
  2.0 37.0 %copy-start.3 = (f32[1,1,1,1024]{3,2,1,0:T(1,128)S(1)}, f32[1,1,1,1024]{3,2,1,0:T(1,128)}, u32[]{:S(2)}) copy-start(f32[1,1,1,1024]{3,2,1,0:T(1,128)} %param.12) | copy-start | bytes 12292
  10.8 39.7 %all-to-all-start = ((s32[1,128,20]{2,0,1:T(1,128)}), s32[1,128,20]{2,0,1:T(1,128)S(1)}, u32[]{:S(2)}, u32[]{:S(2)}) async-start(s32[1,128,20]{2,0,1:T(1,128)} %bitcast.26), calls=%async_computation | async-start | bytes 131072 | tf_op jit(solution)/shard_map/all_to_all | solution.py:112
  30.7 72.8 %collective-permute-start.1 = (f32[11,3,8,128]{3,2,1,0:T(8,128)}, f32[11,3,8,128]{3,2,1,0:T(8,128)S(1)}, u32[]{:S(2)}, u32[]{:S(2)}) collective-permute-start(f32[11,3,8,128]{3,2,1,0:T(8,128)} %get-tuple-element.18), channel_id=1, source_target_pairs={{4,0},{8,4},{12,8},{16,12},{20,16},{24,20},{28,24},{32,28},{36,32}... | collective-permute-start | bytes 405512 | tf_op jit(solution)/shard_map/ppermute | solution.py:19
  32.8 70.7 %collective-permute-start = (f32[11,3,8,128]{3,2,1,0:T(8,128)S(1)}, f32[11,3,8,128]{3,2,1,0:T(8,128)S(1)}, u32[]{:S(2)}, u32[]{:S(2)}) collective-permute-start(f32[11,3,8,128]{3,2,1,0:T(8,128)S(1)} %get-tuple-element.17), channel_id=1, source_target_pairs={{0,4},{4,8},{8,12},{12,16},{16,20},{20,24},{24,28},{28,32},{32,36}... | collective-permute-start | bytes 405512 | tf_op jit(solution)/shard_map/ppermute | solution.py:18
  50.5 60.0 %all-to-all-start.1 = ((f32[5,128,20]{2,0,1:T(8,128)}), f32[5,128,20]{2,0,1:T(8,128)S(1)}, u32[]{:S(2)}, u32[]{:S(2)}) async-start(f32[5,128,20]{2,0,1:T(8,128)} %copy.22), calls=%async_computation.1 | async-start | bytes 1048576 | tf_op jit(solution)/shard_map/all_to_all | solution.py:111
  104.5 98.0 %collective-permute-start.3 = (f32[11,14,3,128]{3,2,1,0:T(4,128)}, f32[11,14,3,128]{3,2,1,0:T(4,128)S(1)}, u32[]{:S(2)}, u32[]{:S(2)}) collective-permute-start(f32[11,14,3,128]{3,2,1,0:T(4,128)} %get-tuple-element.16), channel_id=1, source_target_pairs={{1,0},{2,1},{3,2},{5,4},{6,5},{7,6},{9,8},{10,9},{11,10},{13,12},{... | collective-permute-start | bytes 709640 | tf_op jit(solution)/shard_map/ppermute | solution.py:19
  106.7 95.8 %collective-permute-start.2 = (f32[11,14,3,128]{3,2,1,0:T(4,128)}, f32[11,14,3,128]{3,2,1,0:T(4,128)S(1)}, u32[]{:S(2)}, u32[]{:S(2)}) collective-permute-start(f32[11,14,3,128]{3,2,1,0:T(4,128)} %get-tuple-element.15), channel_id=1, source_target_pairs={{0,1},{1,2},{2,3},{4,5},{5,6},{6,7},{8,9},{9,10},{10,11},{12,13},{... | collective-permute-start | bytes 709640 | tf_op jit(solution)/shard_map/ppermute | solution.py:18
where the time goes:
time: 205 us
  other arithmetic  87.6 us (43%)
  starting transfers between devices  52.5 us (26%)
  blocking collectives  44.9 us (22%)
  local copies, waits for them, and re-layouts  18.7 us (9%)
    scatter-add x1, other arithmetic, local(): source = source.at[:, merged_targets[0]].add(merged_values).reshape(chann...  66.5 us
    all_gather x1, blocking collectives, local(): lax.all_gather(tile_targets, 'sec', axis=1, tiled=True)  27.9 us
    all_to_all x1, starting transfers between devices, local(): lax.all_to_all(packed_values, ('gx', 'gy'), split_axis=1, concat_axis=1,...  23.5 us
    all_to_all x1, starting transfers between devices, local(): lax.all_to_all(packed_targets, ('gx', 'gy'), split_axis=1, concat_axis=1,...  18.3 us
    all_gather x1, blocking collectives, local(): lax.all_gather(tile_values, 'sec', axis=1, tiled=True)  17 us
    scatter x1, other arithmetic, local(): jnp.zeros((channels, buffer_width), jnp.float32).at[:, position]  9.7 us
    unnamed x11, local copies, waits for them, and re-layouts  7.16 us
    ppermute x2, starting transfers between devices, extended(): before = lax.ppermute(last, axis, up)  6.37 us
  transfers between devices with their start and end apart: 6, of which 0 were waited for; matrix products, arithmetic and copies ran while one was open for 46% of the time, Pallas kernels for 0%

commit v1 on v0

--- a/solution.py
+++ b/solution.py
@@ -108,7 +108,15 @@
         jnp.zeros((1, buffer_width), jnp.int32).at[0, position].set(target_cell, mode="drop")
     )
     tile_values, tile_targets = (
-        lax.all_to_all(packed_values, ("gx", "gy"), split_axis=1, concat_axis=1, tiled=True),
+        jnp.concatenate(
+            lax.all_to_all(
+                jnp.stack(jnp.split(packed_values, lax.axis_size(("gx", "gy")), axis=1)),
+                ("gx", "gy"),
+                0,
+                0,
+            ),
+            axis=1,
+        ),
         lax.all_to_all(packed_targets, ("gx", "gy"), split_axis=1, concat_axis=1, tiled=True),
     )
     merged_values, merged_targets = (

time: 205 us -> 314 us (1.53)
  local copies, waits for them, and re-layouts: 18.7 us -> 125 us
    unnamed x11 -> x138, local copies, waits for them, and re-layouts: 7.16 us -> 82.2 us
    split x0 -> x135, local copies, waits for them, and re-layouts: none -> 33.1 us  [local(): jnp.split(packed_values, lax.axis_size(('gx', 'gy')), axis=1)]
  transfers between devices with their start and end apart: 6 -> 6, of which waited for: 0 -> 0; matrix products, arithmetic and copies ran while one was open for 46% -> 64% of each run, Pallas kernels for 0% -> 0%
where the time goes in v1:
time: 314 us; the launch traced here: 312 us
  local copies, waits for them, and re-layouts  125 us (40%)
  other arithmetic  87.5 us (28%)
  starting transfers between devices  52.4 us (17%)
  blocking collectives  45 us (14%)
    unnamed x138, local copies, waits for them, and re-layouts  82.2 us
    scatter-add x1, other arithmetic, local(): source = source.at[:, merged_targets[0]].add(merged_values).reshape(chann...  66.5 us
    split x135, local copies, waits for them, and re-layouts, local(): jnp.split(packed_values, lax.axis_size(('gx', 'gy')), axis=1)  33.1 us
    all_gather x1, blocking collectives, local(): lax.all_gather(tile_targets, 'sec', axis=1, tiled=True)  28.1 us
    all_to_all x1, starting transfers between devices, local(): lax.all_to_all(jnp.stack(jnp.split(packed_values, lax.axis_size(('gx', 'g...  23.5 us
    all_to_all x1, starting transfers between devices, local(): lax.all_to_all(packed_targets, ('gx', 'gy'), split_axis=1, concat_axis=1,...  18.3 us
    all_gather x1, blocking collectives, local(): lax.all_gather(tile_values, 'sec', axis=1, tiled=True)  17 us
    scatter x1, other arithmetic, local(): jnp.zeros((channels, buffer_width), jnp.float32).at[:, position]  9.69 us
  transfers between devices with their start and end apart: 6, of which 0 were waited for; matrix products, arithmetic and copies ran while one was open for 64% of the time, Pallas kernels for 0%

profile of v1, /device:TPU:91, one launch (start us, length us, event | category | flops | bytes accessed | tf_op | source)
XLA Modules:
  0.0 311.6 jit_solution(4669498610223915699)
XLA Ops:
  0.0 0.8 copy.800
  2.1 1.2 fusion.4
  3.3 0.7 compare_select_fusion.2
  4.0 0.7 and_reduce_fusion
  4.8 0.7 fusion.65
  5.5 4.5 %scatter_custom_fusion.2 = s32[2560]{0:T(1024)S(1)} fusion(s32[1024]{0:T(1024)S(1)} %broadcast_select_fusion.3, s32[1024]{0:T(1024)} %bitcast.404, s32[]{:T(128)} %constant.27.clone.1), kind=kCustom, calls=%fused_computation.295 | custom fusion | bytes 10752
  10.0 0.7 all_to_all.11
  10.8 18.3 %all-to-all-start = ((s32[1,128,20]{2,0,1:T(1,128)}), s32[1,128,20]{2,0,1:T(1,128)S(1)}, u32[]{:S(2)}, u32[]{:S(2)}) async-start(s32[1,128,20]{2,0,1:T(1,128)} %bitcast.26), calls=%async_computation | async-start | bytes 131072 | tf_op jit(solution)/shard_map/all_to_all | solution.py:120
  29.1 1.0 pad_maximum_fusion.4
  30.0 2.2 collective-permute-start.1
  32.2 3.1 %collective-permute-start = (f32[11,3,8,128]{3,2,1,0:T(8,128)S(1)}, f32[11,3,8,128]{3,2,1,0:T(8,128)S(1)}, u32[]{:S(2)}, u32[]{:S(2)}) collective-permute-start(f32[11,3,8,128]{3,2,1,0:T(8,128)S(1)} %get-tuple-element.145), channel_id=1, source_target_pairs={{0,4},{4,8},{8,12},{12,16},{16,20},{20,24},{24,28},{28,32},{32,36}... | collective-permute-start | bytes 405512 | tf_op jit(solution)/shard_map/ppermute | solution.py:18
  35.3 2.7 copy.803
  38.0 9.7 %scatter_custom_fusion = f32[5,2560]{0,1:T(8,128)S(1)} fusion(s32[1024]{0:T(1024)S(1)} %bitcast.400, f32[]{:T(128)} %constant.32.clone.1, f32[1024]{0:T(1024)S(1)} %bitcast.403, f32[5,8192]{0,1:T(8,128)} %bitcast.393, s32[1024]{0:T(1024)S(1)} %broadcast_clamp_fusion), kind=kCustom, calls=%fused_computation.7 | custom fusion | flops 5120 | bytes 223236 | tf_op jit(solution)/shard_map/scatter | solution.py:105
  47.8 0.7 fusion.78
  48.5 0.7 fusion.77
  51.1 0.8 copy.818
  51.9 0.8 copy.819
  52.7 0.8 copy.820
  53.5 0.8 copy.821
  54.3 0.8 copy.822
  55.1 0.8 copy.823
  55.9 0.8 copy.824
  56.7 0.8 copy.825
  57.4 0.8 copy.826
  58.2 0.8 copy.827
  59.0 0.8 copy.828
  59.8 0.8 copy.829
  60.6 0.8 copy.830
  61.4 0.8 copy.831
  62.2 0.8 copy.832
  63.0 0.8 copy.833
  63.8 0.8 copy.834
  64.5 0.8 copy.835
  65.3 0.8 copy.836
  66.1 0.8 copy.837
  66.9 0.8 copy.838
  67.7 0.8 copy.839
  68.5 0.8 copy.840
  69.3 0.8 copy.841
  70.1 0.8 copy.842
  70.9 0.8 copy.843
  71.7 0.8 copy.844
  72.4 0.8 copy.845
  73.2 0.8 copy.846
  81.8 0.6 constant_dynamic-update-slice_fusion.152
  88.9 0.6 constant_dynamic-update-slice_fusion.140
  116.7 0.6 constant_dynamic-update-slice_fusion.93
  123.2 0.6 constant_dynamic-update-slice_fusion.82
  144.5 0.6 constant_dynamic-update-slice_fusion.46
  156.2 0.6 constant_dynamic-update-slice_fusion.26
  156.9 23.5 %all-to-all-start.1 = ((f32[128,5,20]{2,1,0:T(8,128)}), f32[128,5,20]{2,1,0:T(8,128)S(1)}, u32[]{:S(2)}, u32[]{:S(2)}) async-start(f32[128,5,20]{2,1,0:T(8,128)} %constant_dynamic-update-slice_fusion.26), calls=%async_computation.1 | async-start | bytes 1048576 | tf_op jit(solution)/shard_map/all_to_all | solution.py:112
  180.9 0.8 reduce.7
  181.8 28.1 %all_gather.6 = s32[1,10240]{1,0:T(1,128)S(1)} all-gather(s32[1,2560]{1,0:T(1,128)S(1)} %all_to_all.13), channel_id=1, replica_groups=mesh['sec'=4,'gx'=32,'gy'=4] {'sec'}, dimensions={1}, use_global_device_ids=true | all-gather | bytes 51200 | tf_op jit(solution)/shard_map/all_gather | solution.py:124
  209.9 0.7 compare_select_fusion
  210.6 0.8 fusion.80
  211.5 2.2 collective-permute-start.3
  213.7 3.1 collective-permute-start.2
  217.5 17.0 %all_gather.7 = f32[5,10240]{1,0:T(8,128)S(1)} all-gather(f32[5,2560]{1,0:T(8,128)S(1)} %reshape.407), channel_id=1, replica_groups=mesh['sec'=4,'gx'=32,'gy'=4] {'sec'}, dimensions={1}, use_global_device_ids=true | all-gather | bytes 256000 | tf_op jit(solution)/shard_map/all_gather | solution.py:123
  234.5 3.1 %copy.933 = f32[10240,5]{1,0:T(8,128)} copy(f32[10240,5]{0,1:T(8,128)S(1)} %bitcast.396) | data formatting | bytes 409600 | tf_op jit(solution)/shard_map/all_gather | solution.py:123
  237.6 66.5 %scatter_custom_fusion.1 = f32[5,8192]{0,1:T(8,128)} fusion(s32[10240]{0:T(1024)} %bitcast.397, f32[10240,5]{1,0:T(8,128)} %copy.933, f32[]{:T(128)} %constant.32.clone.1), kind=kCustom, calls=%fused_computation.5 | custom fusion | flops 51200 | bytes 164352 | tf_op jit(solution)/shard_map/scatter-add | solution.py:129
  304.1 2.3 broadcast_select_fusion
  306.3 2.9 copy.934
  310.0 0.7 add_add_fusion
  310.8 0.7 multiply_add_fusion
  (289 shorter events, 83.8 us)
Async XLA Ops:
  0.0 35.3 %copy-start = (f32[1,5,8,8,128]{4,3,2,1,0:T(8,128)S(1)}, f32[1,5,8,8,128]{4,3,2,1,0:T(8,128)}, u32[]{:S(2)}) copy-start(f32[1,5,8,8,128]{4,3,2,1,0:T(8,128)} %param.7) | copy-start | bytes 491524
  1.5 36.5 %copy-start.2 = (s32[1,1,1,1024]{3,2,1,0:T(1,128)S(1)}, s32[1,1,1,1024]{3,2,1,0:T(1,128)}, u32[]{:S(2)}) copy-start(s32[1,1,1,1024]{3,2,1,0:T(1,128)} %param.9) | copy-start | bytes 12292
  1.5 36.5 %copy-start.3 = (f32[1,1,1,1024]{3,2,1,0:T(1,128)S(1)}, f32[1,1,1,1024]{3,2,1,0:T(1,128)}, u32[]{:S(2)}) copy-start(f32[1,1,1,1024]{3,2,1,0:T(1,128)} %param.12) | copy-start | bytes 12292
  10.8 146.1 %all-to-all-start = ((s32[1,128,20]{2,0,1:T(1,128)}), s32[1,128,20]{2,0,1:T(1,128)S(1)}, u32[]{:S(2)}, u32[]{:S(2)}) async-start(s32[1,128,20]{2,0,1:T(1,128)} %bitcast.26), calls=%async_computation | async-start | bytes 131072 | tf_op jit(solution)/shard_map/all_to_all | solution.py:120
  30.0 180.6 %collective-permute-start.1 = (f32[11,3,8,128]{3,2,1,0:T(8,128)S(1)}, f32[11,3,8,128]{3,2,1,0:T(8,128)S(1)}, u32[]{:S(2)}, u32[]{:S(2)}) collective-permute-start(f32[11,3,8,128]{3,2,1,0:T(8,128)S(1)} %get-tuple-element.146), channel_id=1, source_target_pairs={{4,0},{8,4},{12,8},{16,12},{20,16},{24,20},{28,24},{32,28},{36,32}... | collective-permute-start | bytes 405512 | tf_op jit(solution)/shard_map/ppermute | solution.py:19
  32.2 178.4 %collective-permute-start = (f32[11,3,8,128]{3,2,1,0:T(8,128)S(1)}, f32[11,3,8,128]{3,2,1,0:T(8,128)S(1)}, u32[]{:S(2)}, u32[]{:S(2)}) collective-permute-start(f32[11,3,8,128]{3,2,1,0:T(8,128)S(1)} %get-tuple-element.145), channel_id=1, source_target_pairs={{0,4},{4,8},{8,12},{12,16},{16,20},{20,24},{24,28},{28,32},{32,36}... | collective-permute-start | bytes 405512 | tf_op jit(solution)/shard_map/ppermute | solution.py:18
  38.0 11.2 %copy-start.1 = (f32[1,6,8,8,128]{4,3,2,1,0:T(8,128)S(1)}, f32[1,6,8,8,128]{4,3,2,1,0:T(8,128)}, u32[]{:S(2)}) copy-start(f32[1,6,8,8,128]{4,3,2,1,0:T(8,128)} %param.8) | copy-start | bytes 589828
  156.9 60.4 %all-to-all-start.1 = ((f32[128,5,20]{2,1,0:T(8,128)}), f32[128,5,20]{2,1,0:T(8,128)S(1)}, u32[]{:S(2)}, u32[]{:S(2)}) async-start(f32[128,5,20]{2,1,0:T(8,128)} %constant_dynamic-update-slice_fusion.26), calls=%async_computation.1 | async-start | bytes 1048576 | tf_op jit(solution)/shard_map/all_to_all | solution.py:112
  211.5 97.8 %collective-permute-start.3 = (f32[11,14,3,128]{3,2,1,0:T(4,128)}, f32[11,14,3,128]{3,2,1,0:T(4,128)S(1)}, u32[]{:S(2)}, u32[]{:S(2)}) collective-permute-start(f32[11,14,3,128]{3,2,1,0:T(4,128)} %get-tuple-element.144), channel_id=1, source_target_pairs={{1,0},{2,1},{3,2},{5,4},{6,5},{7,6},{9,8},{10,9},{11,10},{13,12},{... | collective-permute-start | bytes 709640 | tf_op jit(solution)/shard_map/ppermute | solution.py:19
  213.7 95.6 %collective-permute-start.2 = (f32[11,14,3,128]{3,2,1,0:T(4,128)S(1)}, f32[11,14,3,128]{3,2,1,0:T(4,128)S(1)}, u32[]{:S(2)}, u32[]{:S(2)}) collective-permute-start(f32[11,14,3,128]{3,2,1,0:T(4,128)S(1)} %get-tuple-element.143), channel_id=1, source_target_pairs={{0,1},{1,2},{2,3},{4,5},{5,6},{6,7},{8,9},{9,10},{10,11},{12,13},{... | collective-permute-start | bytes 709640 | tf_op jit(solution)/shard_map/ppermute | solution.py:18
